TPU v7x, 32 devices: a whole 2x2x4 slice. The times are simulated.
32 devices in a mesh: beam: 2 (over y), chan: 8 (over z, x), tm: 2 (over core).
Axes of the slice: x: 2, y: 2, z: 4, core: 2. Of those that a mesh axis runs over, the one named last changes fastest.
Arguments:
- spectra: float32 [512, 8192], P(('beam', 'chan'), 'tm'), parts along dimension 0, may hold values from -6 to 6
- delay_shifts: int32 [8, 256], replicated, may hold values from 0 to 112, as said below
- box_widths: int32 [20], replicated, may hold values from 1 to 128, as said below
Outputs:
- pulse_power: float32 [512, 8192], P(('beam', 'chan'), 'tm'), parts along dimension 0
There are 2 independent parts, one for each index of `beam`. A program takes and returns all parts, laid end to end along the dimension named above; an argument that names none is the same for every part. Nothing has to cross between parts.
Inputs may be any that keep to these rules, and one draw needn't show every extreme that they name: `delay_shifts`: each section's row of the table contains 112 in some column. `box_widths`: some filter has width 128.
All inputs are finite; a program needn't handle non-finite values.
Results may differ from a plain program's by a relative error of at most 0.000023.
Values sent between devices are 32-bit elements; how exact they have to be, the bound alone decides.
A program may use at most 64 MiB of HBM per device.

v0:
```python
import jax
import jax.numpy as jnp
from jax import lax
from jax.sharding import PartitionSpec as P

LOCAL_SECTIONS = 5
SWAP_SECTIONS = 3
TAIL = 1024
SHIFT_MAX = 112
WMAX = 128
NBOX = 20


root_half = 0.7071067811865476


def from_behind(x, axis, by):
    peers = lax.axis_size(axis)
    pairs = [(i, i + by) for i in range(peers) if 0 <= i + by < peers]
    return lax.ppermute(x, axis, pairs)


def swapped(block, axis, bit):
    count = lax.axis_size(axis)
    route = []
    for low in range(count):
        high = low | 1 << bit
        if high != low and high < count:
            route += [(low, high), (high, low)]
    return lax.ppermute(block, axis, route)


def pair_rows(series, stride):
    total_rows, length = series.shape
    paired = series.reshape(total_rows // (2 * stride), 2, stride, length)
    lower = jnp.broadcast_to(paired[:, 0:1], paired.shape).reshape(total_rows, length)
    upper = jnp.broadcast_to(paired[:, 1:2], paired.shape).reshape(total_rows, length)
    return (lower, upper)


def delay_add(lower, upper_wide, shifts):
    current = upper_wide
    bit_count = SHIFT_MAX.bit_length()
    for bit_place in range(bit_count):
        amount = 2**bit_place
        moved = jnp.concatenate(
            [jnp.zeros((current.shape[0], amount), current.dtype), current[:, :-amount]], axis=1
        )
        take_moved = (shifts >> bit_place & 1)[:, None] == 1
        current = jnp.where(take_moved, moved, current)
    delayed = current[:, SHIFT_MAX:]
    return (lower + delayed) * root_half


def widen_upper(upper):
    earlier = jnp.zeros((upper.shape[0], SHIFT_MAX), upper.dtype)
    return jnp.concatenate([earlier, upper], axis=1)


def boxcar_power(segment, box_widths):
    length = segment.shape[1] - WMAX
    running = jnp.cumsum(segment, axis=1)
    closing = running[:, WMAX:]

    def add_filter(which, summed):
        span_width = box_widths[which]
        opening = lax.dynamic_slice_in_dim(running, WMAX - span_width, length, 1)
        window_sum = closing - opening
        return summed + window_sum * window_sum / span_width.astype(jnp.float32)

    summed = lax.fori_loop(0, NBOX, add_filter, jnp.zeros(closing.shape, jnp.float32))
    return summed / NBOX


def local(spectra, delay_shifts, box_widths):
    ch_rows, time_len = spectra.shape
    row_start = lax.axis_index("chan") * ch_rows
    own_shifts = lax.dynamic_slice_in_dim(delay_shifts, row_start, ch_rows, 1)
    earlier = from_behind(spectra[:, -TAIL:], "tm", 1)
    series = jnp.concatenate([earlier, spectra], axis=1)
    for level in range(LOCAL_SECTIONS):
        lower, upper = pair_rows(series, 2**level)
        series = delay_add(lower, widen_upper(upper), own_shifts[level])
    chan_bits = lax.axis_size("chan").bit_length() - 1
    for swap_step in range(SWAP_SECTIONS):
        bit_place = chan_bits - SWAP_SECTIONS + swap_step
        partner = swapped(series, "chan", bit_place)
        own_bit = lax.axis_index("chan") >> bit_place & 1
        lower = jnp.where(own_bit == 0, series, partner)
        upper = jnp.where(own_bit == 0, partner, series)
        series = delay_add(lower, widen_upper(upper), own_shifts[LOCAL_SECTIONS + swap_step])
    segment = series[:, TAIL - WMAX :]
    return boxcar_power(segment, box_widths)


def solution(mesh):
    in_specs = (P(("beam", "chan"), "tm"), P(), P())
    out_specs = P(("beam", "chan"), "tm")
    return jax.shard_map(local, mesh=mesh, in_specs=in_specs, out_specs=out_specs, check_vma=False)
```

profile of v0, /device:TPU:0, one launch (start us, length us, event | category | flops | bytes accessed | tf_op | source)
XLA Modules:
  0.0 169.1 jit_solution(4183025125275528850)
XLA Ops:
  0.0 0.9 slice.261
  0.9 2.4 %collective-permute-start = (f32[32,1024]{1,0:T(8,128)S(1)}, f32[32,1024]{1,0:T(8,128)S(1)}, u32[]{:S(2)}, u32[]{:S(2)}) collective-permute-start(f32[32,1024]{1,0:T(8,128)S(1)} %slice.261), channel_id=1, source_target_pairs={{0,1},{2,3},{4,5},{6,7},{8,9},{10,11},{12,13},{14,15},{16,17},{18,... | collective-permute-start | bytes 393224 | tf_op jit(solution)/shard_map/ppermute | solution.py:20
  3.5 0.8 collective-permute-done
  4.3 1.1 pad_maximum_fusion
  22.4 2.4 %collective-permute-start.1 = (f32[32,5120]{1,0:T(8,128)S(1)}, f32[32,5120]{1,0:T(8,128)S(1)}, u32[]{:S(2)}, u32[]{:S(2)}) collective-permute-start(f32[32,5120]{1,0:T(8,128)S(1)} %fusion.5), channel_id=1, source_target_pairs={{0,2},{2,0},{4,6},{6,4},{8,10},{10,8},{12,14},{14,12},{1,3},{3,1},... | collective-permute-start | bytes 1966088 | tf_op jit(solution)/shard_map/ppermute | solution.py:30
  24.8 15.2 %collective-permute-done.1 = f32[32,5120]{1,0:T(8,128)S(1)} collective-permute-done((f32[32,5120]{1,0:T(8,128)S(1)}, f32[32,5120]{1,0:T(8,128)S(1)}, u32[]{:S(2)}, u32[]{:S(2)}) %collective-permute-start.1) | collective-permute-done | bytes 655392 | tf_op jit(solution)/shard_map/ppermute | solution.py:30
  42.4 1.9 %collective-permute-start.2 = (f32[32,5120]{1,0:T(8,128)S(1)}, f32[32,5120]{1,0:T(8,128)S(1)}, u32[]{:S(2)}, u32[]{:S(2)}) collective-permute-start(f32[32,5120]{1,0:T(8,128)S(1)} %fusion.3), channel_id=1, source_target_pairs={{0,4},{4,0},{2,6},{6,2},{8,12},{12,8},{10,14},{14,10},{1,5},{5,1},... | collective-permute-start | bytes 1966088 | tf_op jit(solution)/shard_map/ppermute | solution.py:30
  44.3 14.6 %collective-permute-done.2 = f32[32,5120]{1,0:T(8,128)S(1)} collective-permute-done((f32[32,5120]{1,0:T(8,128)S(1)}, f32[32,5120]{1,0:T(8,128)S(1)}, u32[]{:S(2)}, u32[]{:S(2)}) %collective-permute-start.2) | collective-permute-done | bytes 655392 | tf_op jit(solution)/shard_map/ppermute | solution.py:30
  61.3 2.7 %collective-permute-start.3 = (f32[32,5120]{1,0:T(8,128)S(1)}, f32[32,5120]{1,0:T(8,128)S(1)}, u32[]{:S(2)}, u32[]{:S(2)}) collective-permute-start(f32[32,5120]{1,0:T(8,128)S(1)} %fusion.1), channel_id=1, source_target_pairs={{0,8},{8,0},{2,10},{10,2},{4,12},{12,4},{6,14},{14,6},{1,9},{9,1},... | collective-permute-start | bytes 1966088 | tf_op jit(solution)/shard_map/ppermute | solution.py:30
  63.9 27.9 %collective-permute-done.3 = f32[32,5120]{1,0:T(8,128)S(1)} collective-permute-done((f32[32,5120]{1,0:T(8,128)S(1)}, f32[32,5120]{1,0:T(8,128)S(1)}, u32[]{:S(2)}, u32[]{:S(2)}) %collective-permute-start.3) | collective-permute-done | bytes 655392 | tf_op jit(solution)/shard_map/ppermute | solution.py:30
  94.4 9.3 %reduce-window.6 = f32[32,33,128]{2,1,0:T(8,128)S(1)} reduce-window(f32[32,33,128]{2,1,0:T(8,128)S(1)} %reshape.859, f32[]{:T(128)} %constant.88.clone.1), window={size=1x1x128 pad=0_0x0_0x127_0}, to_apply=%region_0.1 | reduce-window | flops 17166336 | bytes 1081348 | tf_op jit(solution)/shard_map/reduce-window
  105.3 62.9 %while.16 = (s32[]{:T(128)}, f32[32,4096]{1,0:T(8,128)S(1)}, s32[20]{0:T(128)S(1)}, f32[32,4224]{1,0:T(8,128)S(1)}, f32[32,4096]{1,0:T(8,128)S(1)}, /*index=5*/s32[]{:T(128)}, s32[1]{0:T(128)}, s32[]{:T(128)}, s32[1]{0:T(128)}) while((s32[]{:T(128)}, f32[32,4096]{1,0:T(8,128)S(1)}, s32[20]{0:T(128)S(1)}, f32[32,4224]{1,0:T(8,128)S(1)}, ...), condition=%wide.region_3.4_spmd.clone, body=%wide.region_2.3_spmd.clone.sunk | while | flops 655368 | bytes 2097329 | solution.py:71
  108.5 0.7 dynamic_slice.31
  111.6 0.7 dynamic_slice.31
  114.8 0.7 dynamic_slice.31
  117.9 0.7 dynamic_slice.31
  121.1 0.7 dynamic_slice.31
  124.2 0.7 dynamic_slice.31
  127.4 0.7 dynamic_slice.31
  130.5 0.7 dynamic_slice.31
  133.6 0.7 dynamic_slice.31
  136.8 0.7 dynamic_slice.31
  139.9 0.7 dynamic_slice.31
  168.2 0.8 broadcast_multiply_fusion
  (137 shorter events, 39.7 us)
Async XLA Ops:
  0.0 3.3 %copy-start = (s32[8,256]{1,0:T(8,128)S(1)}, s32[8,256]{1,0:T(8,128)}, u32[]{:S(2)}) copy-start(s32[8,256]{1,0:T(8,128)} %param.6) | copy-start | bytes 24580
  0.9 3.3 %collective-permute-start = (f32[32,1024]{1,0:T(8,128)S(1)}, f32[32,1024]{1,0:T(8,128)S(1)}, u32[]{:S(2)}, u32[]{:S(2)}) collective-permute-start(f32[32,1024]{1,0:T(8,128)S(1)} %slice.261), channel_id=1, source_target_pairs={{0,1},{2,3},{4,5},{6,7},{8,9},{10,11},{12,13},{14,15},{16,17},{18,... | collective-permute-start | bytes 393224 | tf_op jit(solution)/shard_map/ppermute | solution.py:20
  22.4 17.6 %collective-permute-start.1 = (f32[32,5120]{1,0:T(8,128)S(1)}, f32[32,5120]{1,0:T(8,128)S(1)}, u32[]{:S(2)}, u32[]{:S(2)}) collective-permute-start(f32[32,5120]{1,0:T(8,128)S(1)} %fusion.5), channel_id=1, source_target_pairs={{0,2},{2,0},{4,6},{6,4},{8,10},{10,8},{12,14},{14,12},{1,3},{3,1},... | collective-permute-start | bytes 1966088 | tf_op jit(solution)/shard_map/ppermute | solution.py:30
  42.4 16.5 %collective-permute-start.2 = (f32[32,5120]{1,0:T(8,128)S(1)}, f32[32,5120]{1,0:T(8,128)S(1)}, u32[]{:S(2)}, u32[]{:S(2)}) collective-permute-start(f32[32,5120]{1,0:T(8,128)S(1)} %fusion.3), channel_id=1, source_target_pairs={{0,4},{4,0},{2,6},{6,2},{8,12},{12,8},{10,14},{14,10},{1,5},{5,1},... | collective-permute-start | bytes 1966088 | tf_op jit(solution)/shard_map/ppermute | solution.py:30
  61.3 30.6 %collective-permute-start.3 = (f32[32,5120]{1,0:T(8,128)S(1)}, f32[32,5120]{1,0:T(8,128)S(1)}, u32[]{:S(2)}, u32[]{:S(2)}) collective-permute-start(f32[32,5120]{1,0:T(8,128)S(1)} %fusion.1), channel_id=1, source_target_pairs={{0,8},{8,0},{2,10},{10,2},{4,12},{12,4},{6,14},{14,6},{1,9},{9,1},... | collective-permute-start | bytes 1966088 | tf_op jit(solution)/shard_map/ppermute | solution.py:30
  104.7 0.7 copy-start.2
  168.2 0.9 copy-start.1
where the time goes:
time: 170 us; the launch traced here: 169 us
  waiting for transfers between devices  58.5 us (34%)
  loops' own time  41.6 us (24%)
  other arithmetic  36.5 us (21%)
  local copies, waits for them, and re-layouts  22.6 us (13%)
  starting transfers between devices  9.32 us (5%)
    ppermute x3, waiting for transfers between devices, swapped(): return lax.ppermute(block, axis, route)  57.7 us
    another operation x1, loops' own time, boxcar_power(): lax.fori_loop(0, NBOX, add_filter, jnp.zeros(closing.shape, jnp.float32))  41.6 us
    select_n x48, other arithmetic, delay_add(): current = jnp.where(take_moved, moved, current)  13.2 us
    dynamic_slice x20, local copies, waits for them, and re-layouts, add_filter(): span_width = box_widths[which]  13.1 us
    another operation x3, other arithmetic  9.77 us
    add x20, other arithmetic, add_filter(): return summed + window_sum * window_sum / span_width.astype(jnp.float32)  8.21 us
    ppermute x3, starting transfers between devices, swapped(): return lax.ppermute(block, axis, route)  6.95 us
  transfers between devices with their start and end apart: 4, of which 4 were waited for; matrix products, arithmetic and copies ran while one was open for 0% of the time, Pallas kernels for 0%

commit v1 on v0

v1 whole, which is shorter than its diff:
```python
import functools

import jax
import jax.numpy as jnp
from jax import lax
from jax.experimental import pallas as pl
from jax.experimental.pallas import tpu as pltpu
from jax.sharding import PartitionSpec as P

SWAPS = 3
LANES = 128
SUB = 8
CHUNKS = 8
MESH = pl.DeviceIdType.MESH


def kernel(shifts_ref, widths_ref, x_ref, out_ref, raw, y, recv, prev, amounts, done, edge, sums,
           load_sem, tail_send, tail_recv, send_sem, recv_sem, hist_send, hist_recv, out_sem):
    rows, time_len = x_ref.shape
    groups = rows // SUB
    levels = rows.bit_length() - 1
    sections = shifts_ref.shape[0]
    boxes = widths_ref.shape[0]
    hist = sections
    tiles = time_len // LANES
    per = tiles // CHUNKS
    chan, tm = lax.axis_index("chan"), lax.axis_index("tm")
    chans, tms = lax.axis_size("chan"), lax.axis_size("tm")
    chan_bits = chans.bit_length() - 1
    bits = [(chan // 2 ** (chan_bits - SWAPS + s)) % 2 for s in range(SWAPS)]
    peers = [chan + (1 - 2 * bits[s]) * 2 ** (chan_bits - SWAPS + s) for s in range(SWAPS)]

    def cols(first, count=1):
        return pl.ds(pl.multiple_of(first * LANES, LANES), count * LANES)

    load = pltpu.make_async_copy(x_ref, raw.at[:, pl.ds(hist * LANES, time_len)], load_sem)
    load.start()

    barrier = pltpu.get_barrier_semaphore()
    for s in range(SWAPS):
        pl.semaphore_signal(barrier, inc=1, device_id={"chan": peers[s]}, device_id_type=MESH)

    @pl.when(tm > 0)
    def _():
        pl.semaphore_signal(barrier, inc=1, device_id={"tm": tm - 1}, device_id_type=MESH)

    sub = lax.broadcasted_iota(jnp.int32, (SUB, LANES), 0)
    lane = lax.broadcasted_iota(jnp.int32, (SUB, LANES), 1)

    def fill(j, _):
        for g in range(groups):
            v = jnp.zeros((SUB, LANES), jnp.int32)
            for r in range(SUB):
                v = jnp.where(sub == r, shifts_ref[j, chan * rows + g * SUB + r], v)
            amounts[j, g * SUB:(g + 1) * SUB, :] = v
        return 0

    lax.fori_loop(0, sections, fill, 0)
    prev[...] = jnp.zeros_like(prev)

    pl.semaphore_wait(barrier, SWAPS + jnp.where(tm < tms - 1, 1, 0))

    def tail():
        return pltpu.make_async_remote_copy(
            src_ref=x_ref.at[:, pl.ds(time_len - hist * LANES, hist * LANES)],
            dst_ref=raw.at[:, pl.ds(0, hist * LANES)],
            send_sem=tail_send, recv_sem=tail_recv,
            device_id={"tm": (tm + 1) % tms}, device_id_type=MESH)

    @pl.when(tm < tms - 1)
    def _():
        tail().start()

    def swap(s, c):
        where = cols(hist + c * per, per)
        return pltpu.make_async_remote_copy(
            src_ref=y.at[s, :, where], dst_ref=recv.at[s, :, where],
            send_sem=send_sem.at[s, c], recv_sem=recv_sem.at[s, c],
            device_id={"chan": peers[s]}, device_id_type=MESH)

    def swap_hist(s):
        first = levels - 1 + s
        where = cols(first, hist - first)
        return pltpu.make_async_remote_copy(
            src_ref=y.at[s, :, where], dst_ref=recv.at[s, :, where],
            send_sem=hist_send.at[s], recv_sem=hist_recv.at[s],
            device_id={"chan": peers[s]}, device_id_type=MESH)

    def delayed(j, g, now, before):
        amount = amounts[j, g * SUB:(g + 1) * SUB, :]
        mixed = jnp.where(lane < LANES - amount, now, before)
        return jnp.take_along_axis(mixed, (lane - amount) & (LANES - 1), axis=1, mode="promise_in_bounds")

    def own_sections(first, count):
        kept = [[prev[j, g * SUB:(g + 1) * SUB, :] for g in range(groups)] for j in range(levels)]
        for t in range(count):
            k = first + t
            v = [raw[g * SUB:(g + 1) * SUB, cols(k)] for g in range(groups)]
            for j in range(levels):
                stride = 2 ** j
                if stride < SUB:
                    high = (sub & stride) != 0
                    low = [jnp.where(high, pltpu.roll(a, stride, 0), a) for a in v]
                    up = [jnp.where(high, a, pltpu.roll(a, SUB - stride, 0)) for a in v]
                else:
                    step = stride // SUB
                    low = [v[g & ~step] for g in range(groups)]
                    up = [v[g | step] for g in range(groups)]
                v = [low[g] + delayed(j, g, up[g], kept[j][g]) for g in range(groups)]
                kept[j] = up
            for g in range(groups):
                y[0, g * SUB:(g + 1) * SUB, cols(k)] = v[g]
        for j in range(levels):
            for g in range(groups):
                prev[j, g * SUB:(g + 1) * SUB, :] = kept[j][g]

    def swap_section(s, first, count, put):
        is_low = bits[s] == 0
        for g in range(groups):
            rs = slice(g * SUB, (g + 1) * SUB)
            before = jnp.where(is_low, recv[s, rs, cols(first - 1)], y[s, rs, cols(first - 1)])
            for t in range(count):
                own, other = y[s, rs, cols(first + t)], recv[s, rs, cols(first + t)]
                up = jnp.where(is_low, other, own)
                low = jnp.where(is_low, own, other)
                put(g, t, low + delayed(levels + s, g, up, before))
                before = up

    def put_next(s, first):
        def put(g, t, value):
            y[s + 1, g * SUB:(g + 1) * SUB, cols(first + t)] = value
        return put

    def put_done(g, t, value):
        done[t * rows + g * SUB:t * rows + (g + 1) * SUB, :] = value

    a = lax.broadcasted_iota(jnp.int32, (LANES, 2 * LANES), 0)
    b = lax.broadcasted_iota(jnp.int32, (LANES, 2 * LANES), 1)
    ones = jnp.where(b < LANES, jnp.where(a <= b, 1.0, 0.0), jnp.where(a > b - LANES, -1.0, 0.0)).astype(jnp.bfloat16)

    def prefixes(x):
        total = None
        for _ in range(3):
            piece = x.astype(jnp.bfloat16)
            part = jnp.dot(piece, ones, preferred_element_type=jnp.float32)
            total = part if total is None else total + part
            x = x - piece.astype(jnp.float32)
        return total

    edge[...] = jnp.zeros_like(edge)

    @pl.when(tm == 0)
    def _():
        for s in range(SWAPS):
            y[s, :, cols(hist - 1)] = jnp.zeros((rows, LANES), jnp.float32)
            recv[s, :, cols(hist - 1)] = jnp.zeros((rows, LANES), jnp.float32)

    load.wait()

    @pl.when(tm > 0)
    def _():
        tail().wait_recv()
        own_sections(0, hist)
        swap_hist(0).start()

    def first_loop(c, _):
        own_sections(hist + c * per, per)
        swap(0, c).start()
        return 0

    lax.fori_loop(0, CHUNKS, first_loop, 0)

    box_lane = lax.broadcasted_iota(jnp.int32, (rows, LANES), 1)
    scale = 0.5 ** sections / boxes

    def out_copy(c):
        where = cols(c * per, per)
        return pltpu.make_async_copy(raw.at[:, where], out_ref.at[:, where], out_sem.at[c])

    def boxcars(c):
        sums[...] = prefixes(done[...])
        for t in range(per):
            now = sums[t * rows:(t + 1) * rows, :LANES]
            before = edge[...] if t == 0 else sums[(t - 1) * rows:t * rows, LANES:]
            power = jnp.zeros((rows, LANES), jnp.float32)
            for f in range(boxes):
                width = widths_ref[f]
                mixed = jnp.where(box_lane < LANES - width, now, before)
                window = now - pltpu.roll(mixed, width & (LANES - 1), 1)
                power = power + window * window * (scale / jnp.full((rows, LANES), width, jnp.int32).astype(jnp.float32))
            raw[:, cols(c * per + t)] = power
        edge[...] = sums[(per - 1) * rows:, LANES:]

    def step(i, _):
        @pl.when(i < CHUNKS)
        def _():
            @pl.when((i == 0) & (tm > 0))
            def _():
                swap_hist(0).wait_recv()
                swap_section(0, levels, hist - levels, put_next(0, levels))
                swap_hist(1).start()
            swap(0, i).wait_recv()
            first = hist + i * per
            swap_section(0, first, per, put_next(0, first))
            swap(1, i).start()

        @pl.when((i >= 1) & (i <= CHUNKS))
        def _():
            c = i - 1
            @pl.when((c == 0) & (tm > 0))
            def _():
                swap_hist(1).wait_recv()
                swap_section(1, levels + 1, hist - levels - 1, put_next(1, levels + 1))
                swap_hist(2).start()
            swap(1, c).wait_recv()
            first = hist + c * per
            swap_section(1, first, per, put_next(1, first))
            swap(2, c).start()

        @pl.when(i >= 2)
        def _():
            c = i - 2
            @pl.when((c == 0) & (tm > 0))
            def _():
                swap_hist(2).wait_recv()
                swap_section(2, hist - 1, 1, put_done)
                edge[...] = prefixes(done[0:rows, :])[:, LANES:]
            swap(2, c).wait_recv()
            swap_section(2, hist + c * per, per, put_done)
            boxcars(c)
            out_copy(c).start()

        return 0

    lax.fori_loop(0, CHUNKS + 2, step, 0)

    def finish(c, _):
        for s in range(SWAPS):
            swap(s, c).wait_send()
        out_copy(c).wait()
        return 0

    lax.fori_loop(0, CHUNKS, finish, 0)

    @pl.when(tm > 0)
    def _():
        for s in range(SWAPS):
            swap_hist(s).wait_send()

    @pl.when(tm < tms - 1)
    def _():
        tail().wait_send()


def local(spectra, delay_shifts, box_widths):
    rows, time_len = spectra.shape
    sections = delay_shifts.shape[0]
    levels = rows.bit_length() - 1
    width = time_len + sections * LANES
    per = time_len // LANES // CHUNKS
    dma = pltpu.SemaphoreType.DMA
    return pl.pallas_call(
        kernel,
        out_shape=jax.ShapeDtypeStruct((rows, time_len), jnp.float32),
        in_specs=[pl.BlockSpec(memory_space=pltpu.SMEM), pl.BlockSpec(memory_space=pltpu.SMEM),
                  pl.BlockSpec(memory_space=pl.ANY)],
        out_specs=pl.BlockSpec(memory_space=pl.ANY),
        scratch_shapes=[
            pltpu.VMEM((rows, width), jnp.float32),
            pltpu.VMEM((SWAPS, rows, width), jnp.float32),
            pltpu.VMEM((SWAPS, rows, width), jnp.float32),
            pltpu.VMEM((levels, rows, LANES), jnp.float32),
            pltpu.VMEM((sections, rows, LANES), jnp.int32),
            pltpu.VMEM((per * rows, LANES), jnp.float32),
            pltpu.VMEM((rows, LANES), jnp.float32),
            pltpu.VMEM((per * rows, 2 * LANES), jnp.float32),
            dma(()), dma(()), dma(()),
            dma((SWAPS, CHUNKS)), dma((SWAPS, CHUNKS)),
            dma((SWAPS,)), dma((SWAPS,)), dma((CHUNKS,)),
        ],
        compiler_params=pltpu.CompilerParams(
            collective_id=0, has_side_effects=True, vmem_limit_bytes=32 * 1024 * 1024),
    )(delay_shifts, box_widths, spectra)


def solution(mesh):
    in_specs = (P(("beam", "chan"), "tm"), P(), P())
    out_specs = P(("beam", "chan"), "tm")
    return jax.shard_map(local, mesh=mesh, in_specs=in_specs, out_specs=out_specs, check_vma=False)
```

time: 170 us -> 51 us (0.30)
  waiting for transfers between devices: 58.5 us -> 0 us
  Pallas kernels: 0 us -> 47.6 us
  loops' own time: 41.6 us -> 0 us
  other arithmetic: 36.5 us -> 0 us
  local copies, waits for them, and re-layouts: 22.6 us -> 3.19 us
  starting transfers between devices: 9.32 us -> 0 us
    ppermute x4 -> x0, waiting for transfers between devices: 58.5 us -> none  [the longest x3 57.7 us: swapped(): return lax.ppermute(block, axis, route)]
    pallas_call x0 -> x1, Pallas kernels: none -> 47.6 us  [local(): pl.pallas_call(kernel, out_shape=jax.ShapeDtypeStruct((rows, time_len), j...]
    another operation x1 -> x0, loops' own time: 41.6 us -> none  [boxcar_power(): lax.fori_loop(0, NBOX, add_filter, jnp.zeros(closing.shape, jnp.float32))]
    select_n x51 -> x0, other arithmetic: 13.4 us -> none  [the longest x48 13.2 us: delay_add(): current = jnp.where(take_moved, moved, current)]
    dynamic_slice x21 -> x0, local copies, waits for them, and re-layouts: 13.2 us -> none  [the longest x20 13.1 us: add_filter(): span_width = box_widths[which]]
    another operation x3 -> x0, other arithmetic: 9.77 us -> none
    ppermute x4 -> x0, starting transfers between devices: 9.32 us -> none  [the longest x3 6.95 us: swapped(): return lax.ppermute(block, axis, route)]
    add x20 -> x0, other arithmetic: 8.21 us -> none  [add_filter(): return summed + window_sum * window_sum / span_width.astype(jnp.float32)]
  transfers between devices with their start and end apart: 4 -> 0, of which waited for: 4 -> 0; matrix products, arithmetic and copies ran while one was open for 0% -> 0% of each run, Pallas kernels for 0% -> 0%
where the time goes in v1:
time: 51 us; the launch traced here: 50.8 us
  Pallas kernels  47.6 us (93%)
  local copies, waits for them, and re-layouts  3.19 us (6%)
    pallas_call x1, Pallas kernels, local(): pl.pallas_call(kernel, out_shape=jax.ShapeDtypeStruct((rows, time_len), j...  47.6 us
    unnamed x7, local copies, waits for them, and re-layouts  3.19 us

profile of v1, /device:TPU:0, one launch (start us, length us, event | category | flops | bytes accessed | tf_op | source)
XLA Modules:
  0.0 50.8 jit_solution(4992048332327073260)
XLA Ops:
  0.0 0.0 copy-start
  0.0 1.0 %copy-done = f32[32,4096]{1,0:T(8,128)S(1)} copy-done((f32[32,4096]{1,0:T(8,128)S(1)}, f32[32,4096]{1,0:T(8,128)}, u32[]{:S(2)}) %copy-start) | copy-done | bytes 524312
  1.0 0.0 copy-start.1
  1.0 0.7 %copy-done.1 = s32[8,256]{1,0:T(8,128)S(1)} copy-done((s32[8,256]{1,0:T(8,128)S(1)}, s32[8,256]{1,0:T(8,128)}, u32[]{:S(2)}) %copy-start.1) | copy-done | bytes 8216
  1.7 0.0 copy-start.2
  1.7 0.7 %copy-done.2 = s32[20]{0:T(128)S(1)} copy-done((s32[20]{0:T(128)S(1)}, s32[20]{0:T(128)}, u32[]{:S(2)}) %copy-start.2) | copy-done | bytes 104
  2.4 47.6 %shard_map.37 = f32[32,4096]{1,0:T(8,128)S(1)} custom-call(s32[8,256]{1,0:T(8,128)S(1)} %copy-done.1, s32[20]{0:T(128)S(1)} %copy-done.2, f32[32,4096]{1,0:T(8,128)S(1)} %copy-done), custom_call_target="tpu_custom_call" | custom-call | tf_op jit(solution)/shard_map/pallas_call | solution.py:262
  50.0 0.8 %copy.5 = f32[32,4096]{1,0:T(8,128)} copy(f32[32,4096]{1,0:T(8,128)S(1)} %shard_map.37) | data formatting | bytes 1048576
Async XLA Ops:
  0.0 1.0 %copy-start = (f32[32,4096]{1,0:T(8,128)S(1)}, f32[32,4096]{1,0:T(8,128)}, u32[]{:S(2)}) copy-start(f32[32,4096]{1,0:T(8,128)} %x_ref.1) | copy-start | bytes 1572868
  1.0 0.7 %copy-start.1 = (s32[8,256]{1,0:T(8,128)S(1)}, s32[8,256]{1,0:T(8,128)}, u32[]{:S(2)}) copy-start(s32[8,256]{1,0:T(8,128)} %shifts_ref.1) | copy-start | bytes 24580
  1.7 0.7 %copy-start.2 = (s32[20]{0:T(128)S(1)}, s32[20]{0:T(128)}, u32[]{:S(2)}) copy-start(s32[20]{0:T(128)} %widths_ref.1) | copy-start | bytes 244

commit v2 on v1

--- a/solution.py
+++ b/solution.py
@@ -116,15 +116,20 @@
 
     def swap_section(s, first, count, put):
         is_low = bits[s] == 0
+        held = []
         for g in range(groups):
             rs = slice(g * SUB, (g + 1) * SUB)
             before = jnp.where(is_low, recv[s, rs, cols(first - 1)], y[s, rs, cols(first - 1)])
+            own = [y[s, rs, cols(first + t)] for t in range(count)]
+            other = [recv[s, rs, cols(first + t)] for t in range(count)]
+            low = [jnp.where(is_low, a, b) for a, b in zip(own, other)]
+            up = [jnp.where(is_low, b, a) for a, b in zip(own, other)]
+            held.append((low, [before] + up))
+        values = [[low[t] + delayed(levels + s, g, up[t + 1], up[t]) for t in range(count)]
+                  for g, (low, up) in enumerate(held)]
+        for g in range(groups):
             for t in range(count):
-                own, other = y[s, rs, cols(first + t)], recv[s, rs, cols(first + t)]
-                up = jnp.where(is_low, other, own)
-                low = jnp.where(is_low, own, other)
-                put(g, t, low + delayed(levels + s, g, up, before))
-                before = up
+                put(g, t, values[g][t])
 
     def put_next(s, first):
         def put(g, t, value):

time: 51 us -> 44.2 us (0.87)
  Pallas kernels: 47.6 us -> 40.8 us
    pallas_call x1, Pallas kernels: 47.6 us -> 40.8 us  [local(): pl.pallas_call(kernel, out_shape=jax.ShapeDtypeStruct((rows, time_len), j...]
where the time goes in v2:
time: 44.2 us; the launch traced here: 44 us
  Pallas kernels  40.8 us (92%)
  local copies, waits for them, and re-layouts  3.19 us (7%)
    pallas_call x1, Pallas kernels, local(): pl.pallas_call(kernel, out_shape=jax.ShapeDtypeStruct((rows, time_len), j...  40.8 us
    unnamed x7, local copies, waits for them, and re-layouts  3.19 us

profile of v2, /device:TPU:0, one launch (start us, length us, event | category | flops | bytes accessed | tf_op | source)
XLA Modules:
  0.0 44.0 jit_solution(18374918682012856284)
XLA Ops:
  0.0 0.0 copy-start
  0.0 1.0 %copy-done = f32[32,4096]{1,0:T(8,128)S(1)} copy-done((f32[32,4096]{1,0:T(8,128)S(1)}, f32[32,4096]{1,0:T(8,128)}, u32[]{:S(2)}) %copy-start) | copy-done | bytes 524312
  1.0 0.0 copy-start.1
  1.0 0.7 %copy-done.1 = s32[8,256]{1,0:T(8,128)S(1)} copy-done((s32[8,256]{1,0:T(8,128)S(1)}, s32[8,256]{1,0:T(8,128)}, u32[]{:S(2)}) %copy-start.1) | copy-done | bytes 8216
  1.7 0.0 copy-start.2
  1.7 0.7 %copy-done.2 = s32[20]{0:T(128)S(1)} copy-done((s32[20]{0:T(128)S(1)}, s32[20]{0:T(128)}, u32[]{:S(2)}) %copy-start.2) | copy-done | bytes 104
  2.4 40.8 %shard_map.37 = f32[32,4096]{1,0:T(8,128)S(1)} custom-call(s32[8,256]{1,0:T(8,128)S(1)} %copy-done.1, s32[20]{0:T(128)S(1)} %copy-done.2, f32[32,4096]{1,0:T(8,128)S(1)} %copy-done), custom_call_target="tpu_custom_call" | custom-call | tf_op jit(solution)/shard_map/pallas_call | solution.py:267
  43.2 0.8 %copy.5 = f32[32,4096]{1,0:T(8,128)} copy(f32[32,4096]{1,0:T(8,128)S(1)} %shard_map.37) | data formatting | bytes 1048576
Async XLA Ops:
  0.0 1.0 %copy-start = (f32[32,4096]{1,0:T(8,128)S(1)}, f32[32,4096]{1,0:T(8,128)}, u32[]{:S(2)}) copy-start(f32[32,4096]{1,0:T(8,128)} %x_ref.1) | copy-start | bytes 1572868
  1.0 0.7 %copy-start.1 = (s32[8,256]{1,0:T(8,128)S(1)}, s32[8,256]{1,0:T(8,128)}, u32[]{:S(2)}) copy-start(s32[8,256]{1,0:T(8,128)} %shifts_ref.1) | copy-start | bytes 24580
  1.7 0.7 %copy-start.2 = (s32[20]{0:T(128)S(1)}, s32[20]{0:T(128)}, u32[]{:S(2)}) copy-start(s32[20]{0:T(128)} %widths_ref.1) | copy-start | bytes 244

commit v3 on v2

--- a/solution.py
+++ b/solution.py
@@ -11,6 +11,7 @@
 LANES = 128
 SUB = 8
 CHUNKS = 8
+LAGS = (1, 2, 4)
 MESH = pl.DeviceIdType.MESH
 
 
@@ -72,17 +73,17 @@
         tail().start()
 
     def swap(s, c):
-        where = cols(hist + c * per, per)
+        where = pl.ds(hist + c * per, per)
         return pltpu.make_async_remote_copy(
-            src_ref=y.at[s, :, where], dst_ref=recv.at[s, :, where],
+            src_ref=y.at[s, where], dst_ref=recv.at[s, where],
             send_sem=send_sem.at[s, c], recv_sem=recv_sem.at[s, c],
             device_id={"chan": peers[s]}, device_id_type=MESH)
 
     def swap_hist(s):
         first = levels - 1 + s
-        where = cols(first, hist - first)
+        where = pl.ds(first, hist - first)
         return pltpu.make_async_remote_copy(
-            src_ref=y.at[s, :, where], dst_ref=recv.at[s, :, where],
+            src_ref=y.at[s, where], dst_ref=recv.at[s, where],
             send_sem=hist_send.at[s], recv_sem=hist_recv.at[s],
             device_id={"chan": peers[s]}, device_id_type=MESH)
 
@@ -109,7 +110,7 @@
                 v = [low[g] + delayed(j, g, up[g], kept[j][g]) for g in range(groups)]
                 kept[j] = up
             for g in range(groups):
-                y[0, g * SUB:(g + 1) * SUB, cols(k)] = v[g]
+                y[0, k, g * SUB:(g + 1) * SUB, :] = v[g]
         for j in range(levels):
             for g in range(groups):
                 prev[j, g * SUB:(g + 1) * SUB, :] = kept[j][g]
@@ -119,9 +120,9 @@
         held = []
         for g in range(groups):
             rs = slice(g * SUB, (g + 1) * SUB)
-            before = jnp.where(is_low, recv[s, rs, cols(first - 1)], y[s, rs, cols(first - 1)])
-            own = [y[s, rs, cols(first + t)] for t in range(count)]
-            other = [recv[s, rs, cols(first + t)] for t in range(count)]
+            before = jnp.where(is_low, recv[s, first - 1, rs, :], y[s, first - 1, rs, :])
+            own = [y[s, first + t, rs, :] for t in range(count)]
+            other = [recv[s, first + t, rs, :] for t in range(count)]
             low = [jnp.where(is_low, a, b) for a, b in zip(own, other)]
             up = [jnp.where(is_low, b, a) for a, b in zip(own, other)]
             held.append((low, [before] + up))
@@ -133,7 +134,7 @@
 
     def put_next(s, first):
         def put(g, t, value):
-            y[s + 1, g * SUB:(g + 1) * SUB, cols(first + t)] = value
+            y[s + 1, first + t, g * SUB:(g + 1) * SUB, :] = value
         return put
 
     def put_done(g, t, value):
@@ -157,8 +158,8 @@
     @pl.when(tm == 0)
     def _():
         for s in range(SWAPS):
-            y[s, :, cols(hist - 1)] = jnp.zeros((rows, LANES), jnp.float32)
-            recv[s, :, cols(hist - 1)] = jnp.zeros((rows, LANES), jnp.float32)
+            y[s, hist - 1] = jnp.zeros((rows, LANES), jnp.float32)
+            recv[s, hist - 1] = jnp.zeros((rows, LANES), jnp.float32)
 
     load.wait()
 
@@ -167,13 +168,6 @@
         tail().wait_recv()
         own_sections(0, hist)
         swap_hist(0).start()
-
-    def first_loop(c, _):
-        own_sections(hist + c * per, per)
-        swap(0, c).start()
-        return 0
-
-    lax.fori_loop(0, CHUNKS, first_loop, 0)
 
     box_lane = lax.broadcasted_iota(jnp.int32, (rows, LANES), 1)
     scale = 0.5 ** sections / boxes
@@ -199,19 +193,25 @@
     def step(i, _):
         @pl.when(i < CHUNKS)
         def _():
-            @pl.when((i == 0) & (tm > 0))
+            own_sections(hist + i * per, per)
+            swap(0, i).start()
+
+        @pl.when((i >= LAGS[0]) & (i < CHUNKS + LAGS[0]))
+        def _():
+            c = i - LAGS[0]
+            @pl.when((c == 0) & (tm > 0))
             def _():
                 swap_hist(0).wait_recv()
                 swap_section(0, levels, hist - levels, put_next(0, levels))
                 swap_hist(1).start()
-            swap(0, i).wait_recv()
-            first = hist + i * per
+            swap(0, c).wait_recv()
+            first = hist + c * per
             swap_section(0, first, per, put_next(0, first))
-            swap(1, i).start()
-
-        @pl.when((i >= 1) & (i <= CHUNKS))
-        def _():
-            c = i - 1
+            swap(1, c).start()
+
+        @pl.when((i >= LAGS[1]) & (i < CHUNKS + LAGS[1]))
+        def _():
+            c = i - LAGS[1]
             @pl.when((c == 0) & (tm > 0))
             def _():
                 swap_hist(1).wait_recv()
@@ -222,9 +222,9 @@
             swap_section(1, first, per, put_next(1, first))
             swap(2, c).start()
 
-        @pl.when(i >= 2)
-        def _():
-            c = i - 2
+        @pl.when(i >= LAGS[2])
+        def _():
+            c = i - LAGS[2]
             @pl.when((c == 0) & (tm > 0))
             def _():
                 swap_hist(2).wait_recv()
@@ -237,7 +237,7 @@
 
         return 0
 
-    lax.fori_loop(0, CHUNKS + 2, step, 0)
+    lax.fori_loop(0, CHUNKS + LAGS[2], step, 0)
 
     def finish(c, _):
         for s in range(SWAPS):
@@ -272,8 +272,8 @@
         out_specs=pl.BlockSpec(memory_space=pl.ANY),
         scratch_shapes=[
             pltpu.VMEM((rows, width), jnp.float32),
-            pltpu.VMEM((SWAPS, rows, width), jnp.float32),
-            pltpu.VMEM((SWAPS, rows, width), jnp.float32),
+            pltpu.VMEM((SWAPS, width // LANES, rows, LANES), jnp.float32),
+            pltpu.VMEM((SWAPS, width // LANES, rows, LANES), jnp.float32),
             pltpu.VMEM((levels, rows, LANES), jnp.float32),
             pltpu.VMEM((sections, rows, LANES), jnp.int32),
             pltpu.VMEM((per * rows, LANES), jnp.float32),
@@ -284,7 +284,7 @@
             dma((SWAPS,)), dma((SWAPS,)), dma((CHUNKS,)),
         ],
         compiler_params=pltpu.CompilerParams(
-            collective_id=0, has_side_effects=True, vmem_limit_bytes=32 * 1024 * 1024),
+            collective_id=0, has_side_effects=True, vmem_limit_bytes=60 * 1024 * 1024),
     )(delay_shifts, box_widths, spectra)
 
 

time: 44.2 us -> 42.8 us (0.968)
  local copies, waits for them, and re-layouts: 3.19 us -> 1.87 us
    unnamed x7 -> x1, local copies, waits for them, and re-layouts: 3.19 us -> 1.87 us
where the time goes in v3:
time: 42.8 us; the launch traced here: 42.6 us
  Pallas kernels  40.8 us (95%)
  local copies, waits for them, and re-layouts  1.87 us (4%)
    pallas_call x1, Pallas kernels, local(): pl.pallas_call(kernel, out_shape=jax.ShapeDtypeStruct((rows, time_len), j...  40.8 us
    unnamed x1, local copies, waits for them, and re-layouts  1.87 us

profile of v3, /device:TPU:0, one launch (start us, length us, event | category | flops | bytes accessed | tf_op | source)
XLA Modules:
  0.0 42.6 jit_solution(6161238851750255146)
XLA Ops:
  0.0 40.8 %shard_map.37 = f32[32,4096]{1,0:T(8,128)} custom-call(s32[8,256]{1,0:T(8,128)} %shifts_ref.1, s32[20]{0:T(128)} %widths_ref.1, f32[32,4096]{1,0:T(8,128)} %x_ref.1), custom_call_target="tpu_custom_call" | custom-call | tf_op jit(solution)/shard_map/pallas_call | solution.py:267
  40.8 1.9 %copy.5 = f32[32,4096]{1,0:T(8,128)} copy(f32[32,4096]{1,0:T(8,128)} %shard_map.37) | data formatting | bytes 1048576

commit v4 on v3

--- a/solution.py
+++ b/solution.py
@@ -10,8 +10,8 @@
 SWAPS = 3
 LANES = 128
 SUB = 8
-CHUNKS = 8
-LAGS = (1, 2, 4)
+CHUNKS = 16
+LAGS = (2, 4, 8)
 MESH = pl.DeviceIdType.MESH
 
 

time: 42.8 us -> 42.4 us (level)
  Pallas kernels: 40.8 us -> 40.3 us
    pallas_call x1, Pallas kernels: 40.8 us -> 40.3 us  [local(): pl.pallas_call(kernel, out_shape=jax.ShapeDtypeStruct((rows, time_len), j...]
where the time goes in v4:
time: 42.4 us; the launch traced here: 42.2 us
  Pallas kernels  40.3 us (95%)
  local copies, waits for them, and re-layouts  1.87 us (4%)
    pallas_call x1, Pallas kernels, local(): pl.pallas_call(kernel, out_shape=jax.ShapeDtypeStruct((rows, time_len), j...  40.3 us
    unnamed x1, local copies, waits for them, and re-layouts  1.87 us

profile of v4, /device:TPU:0, one launch (start us, length us, event | category | flops | bytes accessed | tf_op | source)
XLA Modules:
  0.0 42.2 jit_solution(14594112613270175931)
XLA Ops:
  0.0 40.3 %shard_map.37 = f32[32,4096]{1,0:T(8,128)} custom-call(s32[8,256]{1,0:T(8,128)} %shifts_ref.1, s32[20]{0:T(128)} %widths_ref.1, f32[32,4096]{1,0:T(8,128)} %x_ref.1), custom_call_target="tpu_custom_call" | custom-call | tf_op jit(solution)/shard_map/pallas_call | solution.py:267
  40.3 1.9 %copy.5 = f32[32,4096]{1,0:T(8,128)} copy(f32[32,4096]{1,0:T(8,128)} %shard_map.37) | data formatting | bytes 1048576
